TPU v7x, 32 devices: a whole 2x2x4 slice. The times are simulated.
32 devices in a mesh: dp: 16 (over z, y, x), mp: 2 (over core).
Axes of the slice: x: 2, y: 2, z: 4, core: 2. Of those that a mesh axis runs over, the one named last changes fastest.
Arguments:
- tokens: bfloat16 [16384, 768], P(('dp', 'mp')), may hold values from -6 to 6
- seg_ids: int32 [32, 512], P('dp'), may hold values from 0 to 3, never falling along the last dimension, each value on 1 to 256 neighbouring positions
- fill_len: int32 [32], P('dp'), may hold values from 256 to 512, as said below
- qkv_weight: bfloat16 [768, 3, 768], P(None, None, 'mp'), may hold values from -0.21875 to 0.21875
- qv_bias: float32 [2, 768], P(None, 'mp'), may hold values from -3 to 3
- out_weight: bfloat16 [768, 768], replicated, may hold values from -0.875 to 0.875
- out_bias: float32 [768], replicated, may hold values from -2 to 2
- norm1_gain: float32 [768], replicated, may hold values from 0.1 to 1.9
- norm1_bias: float32 [768], replicated, may hold values from -2 to 2
- in_weight: bfloat16 [768, 3072], replicated, may hold values from -0.21875 to 0.21875
- in_bias: float32 [3072], replicated, may hold values from -3 to 3
- down_weight: bfloat16 [3072, 768], replicated, may hold values from -0.15625 to 0.15625
- down_bias: float32 [768], replicated, may hold values from -2 to 2
- norm2_gain: float32 [768], replicated, may hold values from 0.1 to 1.9
- norm2_bias: float32 [768], replicated, may hold values from -2 to 2
- act_range: float32 [4], replicated, may hold values from 1.5 to 3
- cotangent: bfloat16 [16384, 768], P(('dp', 'mp')), may hold values from -6 to 6
Outputs:
- layer_out: bfloat16 [16384, 768], P(('dp', 'mp'))
- grad_tokens: float32 [16384, 768], P(('dp', 'mp'))
- grad_qkv_weight: float32 [768, 3, 768], P(None, None, ('mp', 'dp'))
- grad_qv_bias: float32 [2, 768], P(None, ('mp', 'dp'))
- grad_out_weight: float32 [768, 768], P(('dp', 'mp'))
- grad_out_bias: float32 [768], P(('dp', 'mp'))
- grad_norm1_gain: float32 [768], P(('dp', 'mp'))
- grad_norm1_bias: float32 [768], P(('dp', 'mp'))
- grad_in_weight: float32 [768, 3072], P(('dp', 'mp'))
- grad_in_bias: float32 [3072], P(('dp', 'mp'))
- grad_down_weight: float32 [3072, 768], P(('dp', 'mp'))
- grad_down_bias: float32 [768], P(('dp', 'mp'))
- grad_norm2_gain: float32 [768], P(('dp', 'mp'))
- grad_norm2_bias: float32 [768], P(('dp', 'mp'))
- new_range: float32 [4], replicated
Inputs may be any that keep to these rules, and one draw needn't show every extreme that they name: `seg_ids`: within a packed row the document numbers never fall; each document covers 1 to 256 positions and some document covers exactly that many. `fill_len`: some packed row is full in every draw.
All inputs are finite; a program needn't handle non-finite values.
Results may differ from a plain program's by a relative error of at most 0.012.
Values may be sent and summed in bfloat16 or wider, within the bound.
A program may use at most 192 MiB of HBM per device.

v0:
```python
from functools import partial

import jax
import jax.numpy as jnp
from jax import lax
from jax.sharding import PartitionSpec as P

HD = 64


EPSILON = 1e-06
MOMENTUM = 0.9


def soft_clip(values_in, clip_limit):
    return clip_limit * jnp.tanh(values_in / clip_limit)


def clip_slope(values_in, clip_limit):
    tangent = jnp.tanh(values_in / clip_limit)
    return 1.0 - tangent * tangent


def norm_forward(hidden, norm_gain, norm_shift):
    center = hidden - jnp.mean(hidden, axis=-1, keepdims=True)
    inv_std = lax.rsqrt(jnp.mean(center * center, axis=-1, keepdims=True) + EPSILON)
    scaled = center * inv_std
    return (scaled * norm_gain + norm_shift, scaled, inv_std)


def norm_backward(upstream, scaled, inv_std, norm_gain):
    weighted = upstream * norm_gain
    centered = weighted - jnp.mean(weighted, axis=-1, keepdims=True)
    centered = centered - scaled * jnp.mean(weighted * scaled, axis=-1, keepdims=True)
    return (inv_std * centered, jnp.sum(upstream * scaled, axis=0), jnp.sum(upstream, axis=0))


def attend_mask(seg_rows, fill_rows):
    positions = jnp.arange(seg_rows.shape[1], dtype=jnp.int32)
    same_doc = seg_rows[:, :, None] == seg_rows[:, None, :]
    live_key = positions[None, None, :] < fill_rows[:, None, None]
    diagonal = positions[:, None] == positions[None, :]
    return same_doc & (live_key | diagonal[None])


def per_device(
    tokens,
    seg_ids,
    fill_len,
    qkv_weight,
    qv_bias,
    out_weight,
    out_bias,
    norm1_gain,
    norm1_bias,
    in_weight,
    in_bias,
    down_weight,
    down_bias,
    norm2_gain,
    norm2_bias,
    act_range,
    cotangent,
):
    low_type = jnp.bfloat16
    wide_type = jnp.float32
    token_float = tokens.astype(wide_type)
    clip_half = soft_clip(token_float, act_range[0]).astype(low_type)
    clip_in = lax.all_gather(clip_half, "mp", axis=0, tiled=True)
    model_width = qkv_weight.shape[0]
    local_width = qkv_weight.shape[2]
    local_heads = local_width // HD
    n_rows, seq_len = seg_ids.shape
    flat_weight = qkv_weight.reshape(model_width, 3 * local_width)
    packed = jnp.dot(clip_in, flat_weight, preferred_element_type=wide_type)
    head_shape = (n_rows, seq_len, local_heads, HD)
    queries = (packed[:, :local_width] + qv_bias[0]).astype(low_type).reshape(head_shape)
    key_rows = packed[:, local_width : 2 * local_width].astype(low_type).reshape(head_shape)
    value_rows = (packed[:, 2 * local_width :] + qv_bias[1]).astype(low_type).reshape(head_shape)
    key_mask = attend_mask(seg_ids, fill_len)[:, None]
    score_scale = HD ** (-0.5)
    scores = (
        jnp.einsum("rqhd,rkhd->rhqk", queries, key_rows, preferred_element_type=wide_type)
        * score_scale
    )
    row_max = jnp.max(jnp.where(key_mask, scores, -1e30), axis=-1, keepdims=True)
    unnormed = jnp.where(key_mask, jnp.exp(jnp.where(key_mask, scores - row_max, -80.0)), 0.0)
    row_sum = jnp.sum(unnormed, axis=-1, keepdims=True)
    log_total = row_max + jnp.log(row_sum)
    probs = (unnormed / row_sum).astype(low_type)
    context = jnp.einsum("rhqk,rkhd->rqhd", probs, value_rows, preferred_element_type=wide_type)
    context = context.reshape(n_rows * seq_len, local_width)
    mixed = soft_clip(context, act_range[1]).astype(low_type)
    mixed_tok = lax.all_to_all(mixed, "mp", split_axis=0, concat_axis=1, tiled=True)
    attn_out = jnp.dot(mixed_tok, out_weight, preferred_element_type=wide_type) + out_bias
    normed, scaled_one, inv_one = norm_forward(token_float + attn_out, norm1_gain, norm1_bias)
    clip_mid = soft_clip(normed, act_range[2]).astype(low_type)
    pre_act = jnp.dot(clip_mid, in_weight, preferred_element_type=wide_type) + in_bias
    activated = jax.nn.gelu(pre_act, approximate=False)
    clip_act = soft_clip(activated, act_range[3]).astype(low_type)
    branch = jnp.dot(clip_act, down_weight, preferred_element_type=wide_type) + down_bias
    result, scaled_two, inv_two = norm_forward(normed + branch, norm2_gain, norm2_bias)
    local_peaks = jnp.stack(
        [
            jnp.max(jnp.abs(token_float)),
            jnp.max(jnp.abs(context)),
            jnp.max(jnp.abs(normed)),
            jnp.max(jnp.abs(activated)),
        ]
    )
    peaks = lax.pmax(local_peaks, ("dp", "mp"))
    new_range = MOMENTUM * act_range + (1.0 - MOMENTUM) * peaks
    d_h2, grad_gain2, grad_shift2 = norm_backward(
        cotangent.astype(wide_type), scaled_two, inv_two, norm2_gain
    )
    d_branch = d_h2.astype(low_type)
    grad_down = jnp.einsum("tf,td->fd", clip_act, d_branch, preferred_element_type=wide_type)
    grad_down_bias = jnp.sum(d_branch.astype(wide_type), axis=0)
    d_act = jnp.einsum("td,fd->tf", d_branch, down_weight, preferred_element_type=wide_type)
    d_act = d_act * clip_slope(activated, act_range[3])
    gelu_value, gelu_back = jax.vjp(partial(jax.nn.gelu, approximate=False), pre_act)
    d_pre = gelu_back(d_act)[0].astype(low_type)
    grad_in = jnp.einsum("td,tf->df", clip_mid, d_pre, preferred_element_type=wide_type)
    grad_in_bias = jnp.sum(d_pre.astype(wide_type), axis=0)
    d_normed = jnp.einsum("tf,df->td", d_pre, in_weight, preferred_element_type=wide_type)
    d_normed = d_h2 + d_normed * clip_slope(normed, act_range[2])
    d_h1, grad_gain1, grad_shift1 = norm_backward(d_normed, scaled_one, inv_one, norm1_gain)
    d_attn = d_h1.astype(low_type)
    grad_out = jnp.einsum("te,td->ed", mixed_tok, d_attn, preferred_element_type=wide_type)
    grad_out_bias = jnp.sum(d_attn.astype(wide_type), axis=0)
    d_mixed_tok = jnp.einsum(
        "td,ed->te", d_attn, out_weight, preferred_element_type=wide_type
    ).astype(low_type)
    d_mixed = lax.all_to_all(d_mixed_tok, "mp", split_axis=1, concat_axis=0, tiled=True)
    d_context = (d_mixed.astype(wide_type) * clip_slope(context, act_range[1])).astype(low_type)
    d_context = d_context.reshape(head_shape)
    re_scores = (
        jnp.einsum("rqhd,rkhd->rhqk", queries, key_rows, preferred_element_type=wide_type)
        * score_scale
    )
    re_probs = jnp.where(key_mask, jnp.exp(jnp.where(key_mask, re_scores - log_total, -80.0)), 0.0)
    probs_low = re_probs.astype(low_type)
    d_values = jnp.einsum(
        "rhqk,rqhd->rkhd", probs_low, d_context, preferred_element_type=wide_type
    ).astype(low_type)
    d_probs = jnp.einsum("rqhd,rkhd->rhqk", d_context, value_rows, preferred_element_type=wide_type)
    row_dot = jnp.sum(re_probs * d_probs, axis=-1, keepdims=True)
    d_scores = (re_probs * (d_probs - row_dot)).astype(low_type)
    d_queries = (
        jnp.einsum("rhqk,rkhd->rqhd", d_scores, key_rows, preferred_element_type=wide_type)
        * score_scale
    ).astype(low_type)
    d_keys = (
        jnp.einsum("rhqk,rqhd->rkhd", d_scores, queries, preferred_element_type=wide_type)
        * score_scale
    ).astype(low_type)
    flat_shape = (n_rows * seq_len, local_width)
    d_packed = jnp.concatenate(
        [d_queries.reshape(flat_shape), d_keys.reshape(flat_shape), d_values.reshape(flat_shape)],
        axis=1,
    )
    grad_qkv = jnp.einsum("tc,tj->cj", clip_in, d_packed, preferred_element_type=wide_type)
    grad_qkv = grad_qkv.reshape(3 * model_width, local_width)
    grad_qv = jnp.stack(
        [
            jnp.sum(d_queries.reshape(flat_shape).astype(wide_type), axis=0),
            jnp.sum(d_values.reshape(flat_shape).astype(wide_type), axis=0),
        ]
    )
    d_clip_in = jnp.einsum("tj,cj->tc", d_packed, flat_weight, preferred_element_type=wide_type)
    d_clip_half = lax.psum_scatter(
        d_clip_in.astype(jnp.bfloat16), "mp", scatter_dimension=0, tiled=True
    ).astype(jnp.float32)
    grad_tokens = d_h1 + d_clip_half * clip_slope(token_float, act_range[0])
    qkv_sum, qv_sum = (
        lax.psum_scatter(grad_qkv, "dp", scatter_dimension=1, tiled=True),
        lax.psum_scatter(grad_qv, "dp", scatter_dimension=1, tiled=True),
    )
    qkv_sum = qkv_sum.reshape(model_width, 3, qkv_sum.shape[1])
    (
        sum_out,
        sum_out_bias,
        sum_gain1,
        sum_shift1,
        sum_in,
        sum_in_bias,
        sum_down,
        sum_down_bias,
        sum_gain2,
        sum_shift2,
    ) = (
        lax.psum_scatter(grad_out, ("dp", "mp"), scatter_dimension=0, tiled=True),
        lax.psum_scatter(grad_out_bias, ("dp", "mp"), scatter_dimension=0, tiled=True),
        lax.psum_scatter(grad_gain1, ("dp", "mp"), scatter_dimension=0, tiled=True),
        lax.psum_scatter(grad_shift1, ("dp", "mp"), scatter_dimension=0, tiled=True),
        lax.psum_scatter(grad_in, ("dp", "mp"), scatter_dimension=0, tiled=True),
        lax.psum_scatter(grad_in_bias, ("dp", "mp"), scatter_dimension=0, tiled=True),
        lax.psum_scatter(grad_down, ("dp", "mp"), scatter_dimension=0, tiled=True),
        lax.psum_scatter(grad_down_bias, ("dp", "mp"), scatter_dimension=0, tiled=True),
        lax.psum_scatter(grad_gain2, ("dp", "mp"), scatter_dimension=0, tiled=True),
        lax.psum_scatter(grad_shift2, ("dp", "mp"), scatter_dimension=0, tiled=True),
    )
    return (
        result.astype(low_type),
        grad_tokens,
        qkv_sum,
        qv_sum,
        sum_out,
        sum_out_bias,
        sum_gain1,
        sum_shift1,
        sum_in,
        sum_in_bias,
        sum_down,
        sum_down_bias,
        sum_gain2,
        sum_shift2,
        new_range,
    )


def solution(mesh):
    return jax.shard_map(
        per_device,
        mesh=mesh,
        in_specs=(
            P(("dp", "mp"), None),
            P("dp", None),
            P("dp"),
            P(None, None, "mp"),
            P(None, "mp"),
            P(),
            P(),
            P(),
            P(),
            P(),
            P(),
            P(),
            P(),
            P(),
            P(),
            P(),
            P(("dp", "mp"), None),
        ),
        out_specs=(
            P(("dp", "mp"), None),
            P(("dp", "mp"), None),
            P(None, None, ("mp", "dp")),
            P(None, ("mp", "dp")),
            P(("dp", "mp"), None),
            P(("dp", "mp")),
            P(("dp", "mp")),
            P(("dp", "mp")),
            P(("dp", "mp"), None),
            P(("dp", "mp")),
            P(("dp", "mp"), None),
            P(("dp", "mp")),
            P(("dp", "mp")),
            P(("dp", "mp")),
            P(),
        ),
        check_vma=False,
    )
```

profile of v0, /device:TPU:0, one launch (start us, length us, event | category | flops | bytes accessed | tf_op | source)
XLA Modules:
  0.0 695.4 jit_solution(4033739095988496220)
XLA Ops:
  7.3 1.4 fusion.54
  8.7 2.9 multiply_convert_fusion.6
  11.6 3.8 copy.62
  16.3 7.9 %all-gather.2.cloned.1.call-done = bf16[1024,768]{1,0:T(8,128)(2,1)} async-done(((bf16[512,768]{1,0:T(8,128)(2,1)}), bf16[1024,768]{1,0:T(8,128)(2,1)}) %all-gather.2.cloned.1.call-update) | async-done | bytes 1572880 | tf_op jit(solution)/shard_map/all_gather | solution.py:69
  24.3 4.2 fusion.57
  28.5 1.4 fusion.20
  30.0 1.4 copy.63
  31.4 1.5 reshape.178
  33.7 1.7 copy.64
  35.4 1.5 reshape.179
  36.9 3.7 select_reduce_fusion
  40.6 3.4 fusion
  44.0 1.1 copy-done.1
  45.2 6.4 abs_reduce_fusion.2
  51.6 4.4 all_to_all.29
  56.0 0.9 fusion.55
  57.3 20.4 %abs_reduce_fusion = (f32[]{:T(128)}, f32[512,3072]{1,0:T(8,128)S(1)}, f32[512,3072]{1,0:T(8,128)S(1)}) fusion(f32[3072]{0:T(1024)S(1)} %copy-done.21, bf16[768,3072]{1,0:T(8,128)(2,1)} %param.26, f32[]{:T(128)} %bitcast.8, f32[768]{0:T(1024)S(1)} %copy-done.30, f32[768]{0:T(1024)S(1)} %copy-done.24, f32[512]{0:T(512)S(1)} %add_rsqrt_fusion.1, ...), kind=kOutput, calls=%fused_computation.9 | convolution fusion | flops 2524053504 | bytes 18896904 | tf_op jit(solution)/shard_map/dot_general | solution.py:98
  77.7 2.3 multiply_convert_fusion.1
  80.1 2.7 fusion.56
  83.2 0.8 fusion.18
  84.0 2.1 convert_reduce_fusion.2
  86.2 8.6 %convert_reduce_fusion = (f32[3072]{0:T(1024)}, bf16[512,3072]{1,0:T(8,128)(2,1)}) fusion(f32[512,3072]{1,0:T(8,128)S(1)} %get-tuple-element.64, f32[]{:T(128)} %bitcast.7, bf16[3072,768]{1,0:T(8,128)(2,1)S(1)} %bitcast.95, f32[512,768]{1,0:T(8,128)S(1)} %get-tuple-element.66, f32[512,3072]{1,0:T(8,128)S(1)} %get-tuple-element.85, f32[3072]{0:T(1024)S(1)} %copy-done.21), kind=kOutput, calls=%fused_computation.10 | convolution fusion | flops 2450912256 | bytes 22044676 | tf_op jit(solution)/shard_map/td,fd->tf/dot_general | solution.py:119
  94.8 8.0 %multiply_reduce_fusion.1 = (f32[768]{0:T(1024)}, f32[512]{0:T(512)S(1)}, f32[]{:T(128)}, f32[512]{0:T(512)S(1)}, f32[768]{0:T(1024)}, /*index=5*/f32[512,768]{1,0:T(8,128)S(1)}) fusion(f32[512]{0:T(512)S(1)} %add_rsqrt_fusion.1, f32[512,768]{1,0:T(8,128)S(1)} %get-tuple-element.84, f32[512]{0:T(512)S(1)} %broadcast_multiply_fusion.5, ...), kind=kOutput, calls=%fused_computation.58 | convolution fusion | flops 2422994432 | bytes 12603400 | tf_op jit(solution)/shard_map/tf,df->td/dot_general | solution.py:125
  102.8 1.1 convert_reduce_fusion.3
  103.9 1.7 convolution_convert_fusion.1
  105.6 2.3 copy.85
  107.9 5.6 all_to_all.30
  113.7 1.2 fusion.21
  114.9 7.3 %convert_reduce_fusion.4 = (f32[6,64]{1,0:T(8,128)}, bf16[2,512,6,64]{1,3,2,0:T(8,128)(2,1)S(1)}) fusion(bf16[2,512,6,64]{1,3,2,0:T(8,128)(2,1)S(1)} %fusion.21, f32[2,6,512]{2,1,0:T(8,128)S(1)} %log_add_fusion, f32[2,6,512,512]{2,3,1,0:T(8,128)} %copy-done.1, pred[2,512,512]{1,2,0:T(8,128)(4,1)S(1)} %or_and_fusion), kind=kOutput, calls=%fused_computation.60 | convolution fusion | flops 419561088 | bytes 14706176 | tf_op jit(solution)/shard_map/rhqk,rqhd->rkhd/dot_general | solution.py:143
  122.3 7.1 %multiply_reduce_fusion = (f32[2,6,512]{2,1,0:T(8,128)S(1)}, f32[2,6,512,512]{2,3,1,0:T(8,128)}) fusion(f32[2,6,512]{2,1,0:T(8,128)S(1)} %log_add_fusion, f32[2,6,512,512]{2,3,1,0:T(8,128)S(1)} %bitcast.78, pred[2,512,512]{1,2,0:T(8,128)(4,1)S(1)} %or_and_fusion, bf16[2,512,6,64]{1,3,2,0:T(8,128)(2,1)S(1)} %fusion.21, bf16[2,512,6,64]{1,0,3,2:T(2,128)(2,1)S(1)} %copy-done.16), kind=kOutput, calls=%fused_computation.1 | convolution fusion | flops 421521408 | bytes 27312128 | tf_op jit(solution)/shard_map/rqhd,rkhd->rhqk/dot_general | solution.py:146
  129.4 7.4 %multiply_convert_fusion = bf16[2,6,512,512]{2,3,1,0:T(8,128)(2,1)S(1)} fusion(f32[2,6,512,512]{2,3,1,0:T(8,128)} %get-tuple-element.90, f32[2,6,512]{2,1,0:T(8,128)S(1)} %get-tuple-element.89, f32[2,6,512]{2,1,0:T(8,128)S(1)} %log_add_fusion, f32[2,6,512,512]{2,3,1,0:T(8,128)S(1)} %bitcast.78, pred[2,512,512]{1,2,0:T(8,128)(4,1)S(1)} %or_and_fusion), kind=kLoop, calls=%fused_computation | loop fusion | flops 22020096 | bytes 32030720 | tf_op jit(solution)/shard_map/convert_element_type | solution.py:148
  136.8 2.0 fusion.29
  138.9 1.2 convert_reduce_fusion.5
  140.1 0.8 copy.79
  141.0 0.8 copy.77
  142.0 0.8 copy.74
  143.1 1.4 copy-done.17
  144.8 3.5 convolution_convert_fusion
  148.3 6.1 fusion.58
  154.4 5.1 reshape.184
  159.5 5.2 copy.86
  164.7 1.1 copy-done.8
  165.8 2.3 fusion.38
  168.4 9.5 %fusion.50 = f32[768,3072]{1,0:T(8,128)} fusion(bf16[512,3072]{1,0:T(8,128)(2,1)} %get-tuple-element.96, f32[]{:T(128)} %bitcast.8, f32[768]{0:T(1024)} %param.25, f32[768]{0:T(1024)} %param.24, f32[512,768]{1,0:T(8,128)} %copy-done.4, f32[512]{0:T(512)} %copy-done.22, f32[512]{0:T(512)S(1)} %broadcast_multiply_fusion.5), kind=kOutput, calls=%fused_computation.126 | convolution fusion | flops 2418671616 | bytes 14166020 | tf_op jit(solution)/shard_map/td,tf->df/dot_general | solution.py:123
  178.0 8.7 %fusion.41 = f32[3072,768]{1,0:T(8,128)} fusion(bf16[512,3072]{1,0:T(8,128)(2,1)} %copy-done.2, f32[512,768]{1,0:T(8,128)} %copy-done.3), kind=kOutput, calls=%fused_computation.117 | convolution fusion | flops 2416312320 | bytes 14155776 | tf_op jit(solution)/shard_map/tf,td->fd/dot_general | solution.py:117
  186.7 1.3 dynamic-slice
  188.7 41.8 %all-reduce.8 = (f32[768]{0:T(1024)}, f32[768]{0:T(1024)}, f32[768]{0:T(1024)}, f32[3072]{0:T(1024)}, f32[768]{0:T(1024)}, /*index=5*/f32[768]{0:T(1024)}, f32[768]{0:T(1024)}) all-reduce(f32[768]{0:T(1024)S(1)} %copy-done.19, f32[768]{0:T(1024)} %get-tuple-element.45, ...), channel_id=6, replica_groups=mesh['dp'=16,'mp'=2] {'dp','mp'}, use_global_device_ids=true, to_apply=%region_18.19.clone | all-reduce | flops 7680 | bytes 61440
  230.5 1.3 dynamic-slice.2
  231.7 1.3 dynamic-slice.3
  233.0 1.3 dynamic-slice.4
  234.2 1.3 dynamic-slice.6
  235.5 1.3 dynamic-slice.7
  236.7 1.3 dynamic-slice.8
  240.1 41.1 %all-reduce = f32[2,384]{1,0:T(2,128)S(1)} all-reduce(f32[2,384]{1,0:T(2,128)S(1)} %pad_maximum_fusion), channel_id=4, replica_groups=mesh['dp'=16,'mp'=2] {'dp'}, use_global_device_ids=true, to_apply=%region_15.16.clone | all-reduce | flops 768 | bytes 6144
  281.8 4.0 fusion.17
  285.9 2.7 pad_maximum_fusion.1
  288.6 1.3 dynamic-slice.5
  289.9 36.8 %pmax.7 = f32[4]{0:T(128)S(1)} all-reduce(f32[4]{0:T(128)S(1)} %pad_maximum_fusion.1), channel_id=1, replica_groups=mesh['dp'=16,'mp'=2] {'dp','mp'}, use_global_device_ids=true, to_apply=%region_37.38 | all-reduce | flops 4 | bytes 32 | tf_op jit(solution)/shard_map/pmax | solution.py:111
  327.2 2.4 copy.87
  329.6 2.1 reshape.185
  331.7 1.2 copy.80
  332.9 72.3 %reduce-scatter.11.cloned.1.call-done = f32[24,768]{1,0:T(8,128)} async-done(((f32[768,768]{1,0:T(8,128)}), f32[24,768]{1,0:T(8,128)}) %reduce-scatter.11.cloned.1.call-update) | async-done | bytes 73744 | tf_op jit(solution)/shard_map/reduce_scatter | solution.py:192
  405.2 140.9 %reduce-scatter.13.cloned.1.call-done = f32[24,3072]{1,0:T(8,128)} async-done(((f32[768,3072]{1,0:T(8,128)}), f32[24,3072]{1,0:T(8,128)}) %reduce-scatter.13.cloned.1.call-update) | async-done | bytes 294928 | tf_op jit(solution)/shard_map/reduce_scatter | solution.py:196
  546.0 142.1 %reduce-scatter.15.cloned.1.call-done = f32[96,768]{1,0:T(8,128)} async-done(((f32[3072,768]{1,0:T(8,128)}), f32[96,768]{1,0:T(8,128)}) %reduce-scatter.15.cloned.1.call-update) | async-done | bytes 294928 | tf_op jit(solution)/shard_map/reduce_scatter | solution.py:198
  (114 shorter events, 7.4 us)
Async XLA Ops:
  7.2 48.7 %copy-start = (bf16[768,768]{1,0:T(8,128)(2,1)S(1)}, bf16[768,768]{1,0:T(8,128)(2,1)}, u32[]{:S(2)}) copy-start(bf16[768,768]{1,0:T(8,128)(2,1)} %param.22) | copy-start | bytes 3538948
  7.2 8.3 %copy-start.26 = (f32[2,384]{1,0:T(2,128)S(1)}, f32[2,384]{1,0:T(2,128)}, u32[]{:S(2)}) copy-start(f32[2,384]{1,0:T(2,128)} %param.21) | copy-start | bytes 9220
  7.2 8.4 %copy-start.27 = (s32[2]{0:T(128)S(1)}, s32[2]{0:T(128)}, u32[]{:S(2)}) copy-start(s32[2]{0:T(128)} %param.19) | copy-start | bytes 28
  7.2 8.5 %copy-start.18 = (s32[2,512]{1,0:T(2,128)S(1)}, s32[2,512]{1,0:T(2,128)}, u32[]{:S(2)}) copy-start(s32[2,512]{1,0:T(2,128)} %param.18) | copy-start | bytes 12292
  7.2 17.0 %all-gather.2.cloned.1.call-start = ((), (), s32[]{:S(2)}) async-start(), calls=%async_computation.7 | async-start | bytes 2359296 | tf_op jit(solution)/shard_map/all_gather | solution.py:69
  11.6 270.2 %reduce-scatter.9.cloned.1.call-start = ((), (), s32[]{:S(2)}) async-start(), calls=%async_computation.8 | async-start | bytes 2359296 | tf_op jit(solution)/shard_map/reduce_scatter | solution.py:171
  33.7 6.9 copy-start.9
  40.6 4.6 copy-start.1
  40.6 4.6 copy-start.15
  45.2 10.8 %copy-start.5 = (bf16[512,768]{1,0:T(8,128)(2,1)S(1)}, bf16[512,768]{1,0:T(8,128)(2,1)}, u32[]{:S(2)}) copy-start(bf16[512,768]{1,0:T(8,128)(2,1)} %param.17) | copy-start | bytes 2359300
  45.2 10.8 %copy-start.28 = (f32[768]{0:T(1024)S(1)}, f32[768]{0:T(1024)}, u32[]{:S(2)}) copy-start(f32[768]{0:T(1024)} %param.23) | copy-start | bytes 9220
  55.9 1.3 copy-start.7
  55.9 1.3 copy-start.21
  55.9 1.3 copy-start.24
  56.0 1.3 copy-start.30
  56.0 24.1 %slice-start.3 = ((s8[4718592]{0:T(1024)(128)(4,1)}), s8[4194304]{0:T(1024)(128)(4,1)S(1)}, s32[]{:S(2)}) async-start(s8[4718592]{0:T(1024)(128)(4,1)} %bitcast.94), calls=%async_computation.16 | async-start | bytes 8388608
  56.9 45.9 %copy-start.4 = (f32[512,768]{1,0:T(8,128)}, f32[512,768]{1,0:T(8,128)S(1)}, u32[]{:S(2)}) copy-start(f32[512,768]{1,0:T(8,128)S(1)} %get-tuple-element.84) | copy-start | bytes 4718596
  57.3 45.5 %copy-start.22 = (f32[512]{0:T(512)}, f32[512]{0:T(512)S(1)}, u32[]{:S(2)}) copy-start(f32[512]{0:T(512)S(1)} %add_rsqrt_fusion.1) | copy-start | bytes 6148
  57.3 22.8 %slice-start.4 = ((s8[4718592]{0:T(1024)(128)(4,1)}), s8[524288]{0:T(1024)(128)(4,1)S(1)}, s32[]{:S(2)}) async-start(s8[4718592]{0:T(1024)(128)(4,1)} %bitcast.94), calls=%async_computation.17 | async-start | bytes 1048576
  77.7 2.4 copy-start.29
  80.1 2.8 copy-start.2
  80.1 3.1 copy-start.11
  80.1 3.1 copy-start.20
  82.9 1.1 copy-start.25
  86.2 8.6 %copy-start.3 = (f32[512,768]{1,0:T(8,128)}, f32[512,768]{1,0:T(8,128)S(1)}, u32[]{:S(2)}) copy-start(f32[512,768]{1,0:T(8,128)S(1)} %get-tuple-element.66) | copy-start | bytes 4718596
  107.9 5.8 copy-start.14
  113.7 8.5 %slice-start = ((s8[12582912]{0:T(1024)(128)(4,1)}), s8[4194304]{0:T(1024)(128)(4,1)S(1)}, s32[]{:S(2)}) async-start(s8[12582912]{0:T(1024)(128)(4,1)} %bitcast.77), calls=%async_computation.13 | async-start | bytes 8388608
  114.9 7.3 %slice-start.1 = ((s8[12582912]{0:T(1024)(128)(4,1)}), s8[4194304]{0:T(1024)(128)(4,1)S(1)}, s32[]{:S(2)}) async-start(s8[12582912]{0:T(1024)(128)(4,1)} %bitcast.77), calls=%async_computation.14 | async-start | bytes 8388608
  114.9 7.3 %slice-start.2 = ((s8[12582912]{0:T(1024)(128)(4,1)}), s8[4194304]{0:T(1024)(128)(4,1)S(1)}, s32[]{:S(2)}) async-start(s8[12582912]{0:T(1024)(128)(4,1)} %bitcast.77), calls=%async_computation.15 | async-start | bytes 8388608
  114.9 7.4 %copy-start.16 = (bf16[2,512,6,64]{1,0,3,2:T(2,128)(2,1)S(1)}, bf16[2,512,6,64]{1,0,3,2:T(2,128)(2,1)}, u32[]{:S(2)}) copy-start(bf16[2,512,6,64]{1,0,3,2:T(2,128)(2,1)} %reshape.178) | copy-start | bytes 2359300
  129.4 7.4 %copy-start.12 = (bf16[2,512,6,64]{1,0,3,2:T(2,128)(2,1)S(1)}, bf16[2,512,6,64]{1,0,3,2:T(2,128)(2,1)}, u32[]{:S(2)}) copy-start(bf16[2,512,6,64]{1,0,3,2:T(2,128)(2,1)} %reshape.179) | copy-start | bytes 2359300
  136.8 2.0 copy-start.10
  142.8 2.0 copy-start.13
  143.1 1.4 copy-start.17
  148.3 179.0 %reduce-scatter.17.cloned.1.call-start = ((), (), s32[]{:S(2)}) async-start(), calls=%async_computation.12 | async-start | bytes 3760128
  164.7 1.1 copy-start.8
  164.7 240.5 %reduce-scatter.11.cloned.1.call-start = ((), (), s32[]{:S(2)}) async-start(), calls=%async_computation.9 | async-start | bytes 2433024 | tf_op jit(solution)/shard_map/reduce_scatter | solution.py:192
  168.1 378.0 %reduce-scatter.13.cloned.1.call-start = ((), (), s32[]{:S(2)}) async-start(), calls=%async_computation.10 | async-start | bytes 9732096 | tf_op jit(solution)/shard_map/reduce_scatter | solution.py:196
  177.9 510.2 %reduce-scatter.15.cloned.1.call-start = ((), (), s32[]{:S(2)}) async-start(), calls=%async_computation.11 | async-start | bytes 9732096 | tf_op jit(solution)/shard_map/reduce_scatter | solution.py:198
  186.7 2.0 copy-start.19
  186.7 95.1 %copy-start.6 = (bf16[512,768]{1,0:T(8,128)(2,1)S(1)}, bf16[512,768]{1,0:T(8,128)(2,1)}, u32[]{:S(2)}) copy-start(bf16[512,768]{1,0:T(8,128)(2,1)} %param.17) | copy-start | bytes 2359300
  230.5 96.2 %copy-start.23 = (f32[4]{0:T(128)S(1)}, f32[4]{0:T(128)}, u32[]{:S(2)}) copy-start(f32[4]{0:T(128)} %param.32) | copy-start | bytes 52
Sparse Core Ops, SparseCore 0:
  11.7 12.4 all-gather.1
  148.4 10.2 reduce-scatter.8
  164.8 135.6 reduce-scatter.16
  307.1 98.0 reduce-scatter.10
  411.5 134.4 reduce-scatter.12
  553.4 134.7 reduce-scatter.14
where the time goes:
time: 704 us; the launch traced here: 695 us
  waiting for transfers between devices  363 us (52%)
  blocking collectives  130 us (18%)
  matrix products  104 us (15%)
  local copies, waits for them, and re-layouts  49.6 us (7%)
  other arithmetic  32.2 us (5%)
  between operations  15.8 us (2%)
    reduce_scatter x1, waiting for transfers between devices, per_device(): lax.psum_scatter(grad_down, ('dp', 'mp'), scatter_dimension=0, tiled=True)  142 us
    reduce_scatter x1, waiting for transfers between devices, per_device(): lax.psum_scatter(grad_in, ('dp', 'mp'), scatter_dimension=0, tiled=True)  141 us
    unnamed x2, blocking collectives  82.8 us
    reduce_scatter x1, waiting for transfers between devices, per_device(): lax.psum_scatter(grad_out, ('dp', 'mp'), scatter_dimension=0, tiled=True)  72.3 us
    pmax x1, blocking collectives, per_device(): peaks = lax.pmax(local_peaks, ('dp', 'mp'))  36.8 us
    unnamed x90, local copies, waits for them, and re-layouts  27.8 us
    dot_general x1, matrix products, per_device(): jnp.dot(clip_mid, in_weight, preferred_element_type=wide_type) + in_bias  20.4 us
  transfers between devices with their start and end apart: 6, of which 4 were waited for; matrix products, arithmetic and copies ran while one was open for 10% of the time, Pallas kernels for 0%

commit v1 on v0

v1 whole, which is shorter than its diff:
```python
import functools
import math

import jax
import jax.numpy as jnp
from jax import lax
from jax.experimental import pallas as pl
from jax.experimental.pallas import tpu as pltpu
from jax.sharding import PartitionSpec as P

HD = 64
EPSILON = 1e-06
MOMENTUM = 0.9
SQRT_HALF = math.sqrt(0.5)
INV_SQRT_2PI = 1.0 / math.sqrt(2.0 * math.pi)
LOW = jnp.bfloat16
WIDE = jnp.float32
MESH = pl.DeviceIdType.MESH

ORDER_A, ORDER_B, ORDER_C = (0, 1, 2, 3), (1, 0, 2, 3), (2, 3, 0, 1)
MESSAGES = (
    ("down", 0, ORDER_A),
    ("down", 1, ORDER_B),
    ("down", 2, ORDER_C),
    ("wide", 0, ORDER_A),
    ("wide", 1, ORDER_B),
    ("wide", 2, ORDER_A),
    ("wide", 3, ORDER_B),
    ("wide", 4, ORDER_C),
    ("wide", 5, ORDER_A),
    ("wide", 6, ORDER_B),
    ("wide", 7, ORDER_A),
)
N_MSG = len(MESSAGES)
DOWN0, IN0, OUT0, QKV0 = 0, 3, 7, 8


def dot(a, b):
    return lax.dot_general(a, b, (((1,), (0,)), ((), ())), preferred_element_type=WIDE)


def dot_nt(a, b):
    return lax.dot_general(a, b, (((1,), (1,)), ((), ())), preferred_element_type=WIDE)


def dot_tn(a, b):
    return lax.dot_general(a, b, (((0,), (0,)), ((), ())), preferred_element_type=WIDE)


def place(chunk, order):
    spot = 0
    for bit in order:
        spot = spot * 2 + (chunk >> bit) % 2
    return spot


class Scatter:
    def __init__(self, n_low, acc, csend, crecv, recvs, send_sem, recv_sem):
        self.acc, self.csend, self.crecv, self.recvs = acc, csend, crecv, recvs
        self.send_sem, self.recv_sem = send_sem, recv_sem
        self.dp, self.mp = lax.axis_index("dp"), lax.axis_index("mp")
        self.n_low = n_low
        self.slot_user = {}
        self.pending = []
        self.next = {}

    def bit(self, bit):
        return (self.dp // (self.n_low << bit)) % 2

    def partner(self, bit):
        return (self.dp + (self.n_low << bit) * (1 - 2 * self.bit(bit)), self.mp)

    def slot(self, m):
        group, index, _ = MESSAGES[m]
        return self.csend[group].at[index % 2]

    def core_copy(self, m):
        group, index, _ = MESSAGES[m]
        return pltpu.make_async_remote_copy(
            src_ref=self.slot(m),
            dst_ref=self.crecv[group].at[index],
            send_sem=self.send_sem.at[m, 0],
            recv_sem=self.recv_sem.at[m, 0],
            device_id=(self.dp, 1 - self.mp),
            device_id_type=MESH,
        )

    def base(self, m, stage):
        order = MESSAGES[m][2]
        spot = 0
        for k in range(stage):
            spot = spot + self.bit(order[k]) * (8 >> k)
        return spot

    def copy(self, m, stage):
        group, index, order = MESSAGES[m]
        count = 16 >> stage
        bit = order[stage - 1]
        start = self.base(m, stage - 1) + (1 - self.bit(bit)) * count
        return pltpu.make_async_remote_copy(
            src_ref=self.acc[group].at[index, pl.ds(start, count)],
            dst_ref=self.recvs[group][stage - 1].at[index],
            send_sem=self.send_sem.at[m, stage],
            recv_sem=self.recv_sem.at[m, stage],
            device_id=self.partner(bit),
            device_id_type=MESH,
        )

    def slot_free(self, m):
        group, index, _ = MESSAGES[m]
        old = self.slot_user.get((group, index % 2))
        if old is not None:
            self.core_copy(old).wait_send()
            self.pending.remove((old, 0))
        self.slot_user[(group, index % 2)] = m

    def send_core(self, m):
        self.core_copy(m).start()
        self.pending.append((m, 0))
        self.next[m] = 0

    def add(self, m, received, from_, start, count):
        group, index, _ = MESSAGES[m]
        acc = self.acc[group]
        here = pl.ds(start, count)
        acc[index, here] = acc[index, here] + received[index, pl.ds(from_, count)]

    def step(self, m, stage, out=None):
        group, index, order = MESSAGES[m]
        assert self.next[m] == stage
        self.next[m] = stage + 1
        (self.core_copy(m) if stage == 0 else self.copy(m, stage)).wait_recv()
        if stage == 4:
            total = self.acc[group][index, self.base(m, 4)].astype(WIDE) + self.recvs[group][3][index, 0].astype(WIDE)
            out(total)
            return
        received = self.crecv[group] if stage == 0 else self.recvs[group][stage - 1]
        count = 8 >> stage
        base = self.base(m, stage)
        mine = self.bit(order[stage])
        self.add(m, received, (1 - mine) * count, base + (1 - mine) * count, count)
        self.copy(m, stage + 1).start()
        self.pending.append((m, stage + 1))
        self.add(m, received, mine * count, base + mine * count, count)

    def finish(self):
        for m, stage in self.pending:
            (self.core_copy(m) if stage == 0 else self.copy(m, stage)).wait_send()


def store_down(ref, first, result, order):
    for chunk in range(16):
        ref[(*first, place(chunk, order))] = result[32 * chunk : 32 * chunk + 32].astype(LOW)


def store_wide(ref, first, result, order):
    half = result.shape[1] // 2
    for chunk in range(16):
        rows = result[24 * chunk : 24 * chunk + 24]
        ref[(*first, place(chunk, order))] = jnp.concatenate([rows[:, :half], rows[:, half:]], axis=0).astype(LOW)


def interleave(ref, values):
    for part in range(2):
        flipped = values(part).T
        for core in range(2):
            groups = [flipped[24 * i : 24 * i + 24] for i in range(core, 16, 2)]
            ref[core, 192 * part : 192 * part + 192, :] = jnp.concatenate(groups, axis=0).astype(LOW)


def kernel(
    n_dp, n_low, upto,
    tok_h, seg_v, fill_s, qkvw_h, qvb_v, outw_h, outb_v, g1_v, b1_v, inw_h, inb_v, downw_h, downb_v, g2_v, b2_v, act_v, cot_h,
    lay_h, gtok_h, gqkv, gout, gin, gdown, small_o,
    tok, cot, wqkv, qvb, wout, win, wdown, clip_in, qkv, bias, ctx, stats, mixed_t, xhat1, clip_mid, clip_mid_t, clip_act_t, slope_f, h2, d_h1, sm, sm_r,
    acc_d, acc_w, cs_d, cs_w, cr_d, cr_w, rd1, rd2, rd3, rd4, rw1, rw2, rw3, rw4,
    loc_sem, wsend, wrecv, msend, mrecv, ssend, srecv,
):
    dp, mp = lax.axis_index("dp"), lax.axis_index("mp")
    n_bits = n_dp.bit_length() - 1
    tokens, width = tok.shape
    hidden = win.shape[1]
    half = width // 2
    other = 1 - mp
    core_id = (dp, other)

    local = [
        pltpu.make_async_copy(src, dst, loc_sem.at[i])
        for i, (src, dst) in enumerate(
            ((tok_h, tok), (qkvw_h, wqkv.at[mp]), (outw_h, wout), (inw_h, win), (downw_h, wdown), (cot_h, cot))
        )
    ]
    for copy in local[:2]:
        copy.start()

    def dp_partner(b):
        return (dp + (1 << b) * (1 - 2 * ((dp // (1 << b)) % 2)), mp)

    barrier = pltpu.get_barrier_semaphore()
    partners = [core_id] + [dp_partner(b) for b in range(n_bits)]
    for there in partners:
        pl.semaphore_signal(barrier, inc=1, device_id=there, device_id_type=MESH)
    for copy in local[2:]:
        copy.start()

    r0, r1, r2, r3 = (act_v[0:1, i : i + 1] for i in range(4))
    i0, i1, i2, i3 = (1.0 / r for r in (r0, r1, r2, r3))

    row = jnp.sum(jnp.where(lax.broadcasted_iota(jnp.int32, seg_v.shape, 0) == mp, seg_v[...], 0), axis=0, keepdims=True).astype(WIDE)
    fill = fill_s[mp]
    seg_col = jnp.broadcast_to(row, (128, tokens)).T[:, 0:1]
    blk = 128

    for i in range(tokens // blk):
        kpos = lax.broadcasted_iota(jnp.int32, (blk, tokens), 1)
        qpos = lax.broadcasted_iota(jnp.int32, (blk, tokens), 0) + i * blk
        live = (kpos < fill) | (kpos == qpos)
        same = seg_col[i * blk : i * blk + blk] == row
        bias[i * blk : i * blk + blk, :] = jnp.where(same & live, 0.0, -1e30)

    pl.semaphore_wait(barrier, len(partners))
    weight_copies = [
        pltpu.make_async_remote_copy(
            src_ref=src, dst_ref=dst, send_sem=wsend.at[i], recv_sem=wrecv.at[i], device_id=core_id, device_id_type=MESH
        )
        for i, (src, dst) in enumerate(((qkvw_h, wqkv.at[mp]), (qvb_v, qvb.at[mp])))
    ]
    for copy in weight_copies:
        copy.start()
    qvb[mp] = qvb_v[...]

    local[0].wait()
    rb = 64
    def rows_at(i, size=rb):
        return pl.ds(pl.multiple_of(i * size, size), size)

    def clip_rows(i, peak):
        v = tok[rows_at(i), :].astype(WIDE)
        clip_in[rows_at(i), :] = (r0 * jnp.tanh(v * i0)).astype(LOW)
        return jnp.maximum(peak, jnp.max(jnp.abs(v), axis=0, keepdims=True))

    peak0 = lax.fori_loop(0, tokens // rb, clip_rows, jnp.zeros((1, width), WIDE))
    stats[...] = jnp.zeros_like(stats)
    lane = lax.broadcasted_iota(jnp.int32, (1, 128), 1)
    in_head = [lane < HD, lane >= HD]
    qb = 256

    def project(part):
        for j in range(3):
            out = dot(clip_in[...], wqkv[part, j])
            if j == 0:
                out = (out + qvb[part, 0:1, :]).astype(LOW).astype(WIDE) * (HD ** -0.5)
            elif j == 2:
                out = out + qvb[part, 1:2, :]
            qkv[j, part] = out.astype(LOW)

    def attend(part):
        def pair(t, carry):
            at = pl.ds(pl.multiple_of(t * 128, 128), 128)
            k, v = qkv[1, part, :, at], qkv[2, part, :, at]
            for i in range(tokens // qb):
                rows = pl.ds(i * qb, qb)
                q = qkv[0, part, rows, at]
                total = jnp.zeros((qb, 128), WIDE)
                found = stats[rows, :]
                for h in range(2):
                    kz = jnp.where(in_head[h], k, jnp.zeros_like(k))
                    vz = jnp.where(in_head[h], v, jnp.zeros_like(v))
                    s = dot_nt(q, kz) + bias[rows, :]
                    top = jnp.max(s, axis=-1, keepdims=True)
                    e = jnp.exp(s - top)
                    norm = jnp.sum(e, axis=-1, keepdims=True)
                    total = total + dot(e.astype(LOW), vz) * (1.0 / norm)
                    found = jnp.where(lane == (part * 6 + t * 2 + h), top + jnp.log(norm), found)
                stats[rows, :] = found
                ctx[rows, pl.ds(pl.multiple_of(part * half + t * 128, 128), 128)] = total
            return carry

        lax.fori_loop(0, half // 128, pair, 0)

    local[1].wait()
    project(mp)
    attend(mp)
    for copy in weight_copies:
        copy.wait()
    project(other)
    attend(other)

    local[2].wait()

    def mix_rows(i, peak):
        c = ctx[rows_at(i), :]
        clip_mid[rows_at(i), :] = (r1 * jnp.tanh(c * i1)).astype(LOW)
        return jnp.maximum(peak, jnp.max(jnp.abs(c), axis=0, keepdims=True))

    peak1 = lax.fori_loop(0, tokens // rb, mix_rows, jnp.zeros((1, width), WIDE))
    interleave(mixed_t, lambda part: clip_mid[:, half * part : half * part + half].astype(WIDE))
    h2[...] = dot(clip_mid[...], wout[...])

    def norm(v):
        center = v - jnp.mean(v, axis=-1, keepdims=True)
        inv = lax.rsqrt(jnp.mean(center * center, axis=-1, keepdims=True) + EPSILON)
        return center * inv, inv

    def norm1_rows(i, peak):
        rows = rows_at(i)
        xhat, inv = norm(tok[rows, :].astype(WIDE) + (h2[rows, :] + outb_v[...]))
        xhat1[rows, :] = xhat
        stats[rows, :] = jnp.where(lane == 127, inv, stats[rows, :])
        normed = xhat * g1_v[...] + b1_v[...]
        h2[rows, :] = normed + downb_v[...]
        clip_mid[rows, :] = (r2 * jnp.tanh(normed * i2)).astype(LOW)
        return jnp.maximum(peak, jnp.max(jnp.abs(normed), axis=0, keepdims=True))

    peak2 = lax.fori_loop(0, tokens // rb, norm1_rows, jnp.zeros((1, width), WIDE))
    interleave(clip_mid_t, lambda part: clip_mid[:, half * part : half * part + half].astype(WIDE))

    local[3].wait()
    local[4].wait()
    fb = 256

    def feed(b, peak):
        cols = pl.ds(pl.multiple_of(b * fb, fb), fb)
        pre = dot(clip_mid[...], win[:, cols]) + inb_v[:, cols]
        u = jnp.abs(pre)
        bell = jnp.exp(pre * pre * -0.5)
        t = 1.0 / (1.0 + (0.3275911 * SQRT_HALF) * u)
        poly = ((((1.061405429 * t - 1.453152027) * t + 1.421413741) * t - 0.284496736) * t + 0.254829592) * t
        tail = 0.5 * poly * bell
        phi_cdf = jnp.where(pre < 0, tail, 1.0 - tail)
        act = pre * phi_cdf
        th = jnp.tanh(act * i3)
        out = (r3 * th).astype(LOW)
        slope_f[:, cols] = ((1.0 - th * th) * (phi_cdf + pre * bell * INV_SQRT_2PI)).astype(LOW)
        flipped = out.T
        for i in range(fb // 32):
            group = b * (fb // 32) + i
            owner = group // 3
            clip_act_t[owner % 2, group % 3, owner // 2] = flipped[32 * i : 32 * i + 32]
        h2[...] += dot(out, wdown[pl.ds(pl.multiple_of(b * fb, fb), fb), :])
        return jnp.maximum(peak, jnp.max(jnp.abs(act), axis=0, keepdims=True))

    peak3 = lax.fori_loop(0, hidden // fb, feed, jnp.zeros((1, fb), WIDE))

    local[5].wait()
    zero_row = jnp.zeros((1, width), WIDE)

    def norm2_rows(i, sums):
        rows = rows_at(i)
        xhat, inv = norm(h2[rows, :])
        e = cot[rows, :].astype(WIDE)
        clip_in_row = (xhat * g2_v[...] + b2_v[...]).astype(LOW)
        clip_mid[rows, :] = clip_in_row
        w = e * g2_v[...]
        d = inv * (w - jnp.mean(w, axis=-1, keepdims=True) - xhat * jnp.mean(w * xhat, axis=-1, keepdims=True))
        h2[rows, :] = d
        low = d.astype(LOW)
        cot[rows, :] = low
        return (
            sums[0] + jnp.sum(e * xhat, axis=0, keepdims=True),
            sums[1] + jnp.sum(e, axis=0, keepdims=True),
            sums[2] + jnp.sum(low.astype(WIDE), axis=0, keepdims=True),
        )

    gain2, shift2, down_bias = lax.fori_loop(0, tokens // rb, norm2_rows, (zero_row, zero_row, zero_row))
    lay_copy = pltpu.make_async_copy(clip_mid, lay_h, loc_sem.at[6])
    lay_copy.start()

    sm[...] = jnp.zeros_like(sm)
    sm[7:8, :] = down_bias
    sm[8:9, :] = gain2
    sm[9:10, :] = shift2
    lane_w = lax.broadcasted_iota(jnp.int32, (1, width), 1)
    peaks = zero_row
    for i, peak in enumerate((peak0, peak1, peak2, peak3)):
        peaks = jnp.where(lane_w == i, jnp.max(peak, axis=-1, keepdims=True), peaks)
    sm[12:13, :] = peaks

    scatter = Scatter(
        n_low,
        {"down": acc_d, "wide": acc_w},
        {"down": cs_d, "wide": cs_w},
        {"down": cr_d, "wide": cr_w},
        {"down": (rd1, rd2, rd3, rd4), "wide": (rw1, rw2, rw3, rw4)},
        msend,
        mrecv,
    )

    def out_down(index):
        def write(total):
            gdown[32 * index : 32 * index + 32, :] = total
        return write

    def out_wide(ref, at):
        def write(total):
            both = jnp.concatenate([total[:24], total[24:]], axis=1)
            if ref is gqkv:
                ref[at] = both
            else:
                ref[:, width * at : width * at + width] = both
        return write

    outs = [out_down(i) for i in range(3)] + [out_wide(gin, i) for i in range(4)] + [out_wide(gout, 0)] + [out_wide(gqkv, i) for i in range(3)]

    def step(m, stage):
        scatter.step(m, stage, outs[m])

    def drain():
        for stage in (0, 1, 2, 3, 4):
            for m in range(N_MSG):
                if scatter.next.get(m) == stage:
                    step(m, stage)
        scatter.finish()

    if upto >= 1:
        for i in range(3):
            m = DOWN0 + i
            order = MESSAGES[m][2]
            scatter.slot_free(m)
            store_down(cs_d, (i % 2,), dot(clip_act_t[other, i].reshape(16 * 32, tokens), cot[...]), order)
            scatter.send_core(m)
            store_down(acc_d, (i,), dot(clip_act_t[mp, i].reshape(16 * 32, tokens), cot[...]), order)
            step(m, 0)

    d_in_bias = []
    if upto >= 2:
        for i in range(4):
            m = IN0 + i
            order = MESSAGES[m][2]
            cols = slice(width * i, width * i + width)
            d_pre = (dot_nt(cot[...], wdown[cols, :]) * slope_f[:, cols].astype(WIDE)).astype(LOW)
            sm[3 + i : 4 + i, :] = jnp.sum(d_pre.astype(WIDE), axis=0, keepdims=True)
            scatter.slot_free(m)
            store_wide(cs_w, (i % 2,), dot(clip_mid_t[other], d_pre), order)
            scatter.send_core(m)
            store_wide(acc_w, (i,), dot(clip_mid_t[mp], d_pre), order)
            back = dot_nt(d_pre, win[:, cols])
            if i == 0:
                d_h1[...] = back
            else:
                d_h1[...] += back
            step(m, 0)

    if upto >= 3:
        lay_copy.wait()
        step(DOWN0, 1)

        def norm1_back(i, sums):
            rows = rows_at(i)
            xhat = xhat1[rows, :]
            inv = stats[rows, 127:128]
            th = jnp.tanh((xhat * g1_v[...] + b1_v[...]) * i2)
            e = h2[rows, :] + d_h1[rows, :] * (1.0 - th * th)
            w = e * g1_v[...]
            d = inv * (w - jnp.mean(w, axis=-1, keepdims=True) - xhat * jnp.mean(w * xhat, axis=-1, keepdims=True))
            d_h1[rows, :] = d
            low = d.astype(LOW)
            cot[rows, :] = low
            return (
                sums[0] + jnp.sum(e * xhat, axis=0, keepdims=True),
                sums[1] + jnp.sum(e, axis=0, keepdims=True),
                sums[2] + jnp.sum(low.astype(WIDE), axis=0, keepdims=True),
            )

        gain1, shift1, out_bias = lax.fori_loop(0, tokens // rb, norm1_back, (zero_row, zero_row, zero_row))
        sm[0:1, :] = out_bias
        sm[1:2, :] = gain1
        sm[2:3, :] = shift1
        order = MESSAGES[OUT0][2]
        scatter.slot_free(OUT0)
        store_wide(cs_w, (0,), dot(mixed_t[other], cot[...]), order)
        scatter.send_core(OUT0)
        store_wide(acc_w, (4,), dot(mixed_t[mp], cot[...]), order)
        h2[...] = dot_nt(cot[...], wout[...])

        def context_rows(i, carry):
            rows = rows_at(i)
            th = jnp.tanh(ctx[rows, :] * i1)
            clip_mid[rows, :] = (h2[rows, :].astype(LOW).astype(WIDE) * (1.0 - th * th)).astype(LOW)
            return carry

        lax.fori_loop(0, tokens // rb, context_rows, 0)
        step(OUT0, 0)

    def attend_back(part):
        def pair(t, carry):
            at = pl.ds(pl.multiple_of(t * 128, 128), 128)
            wide_at = pl.ds(pl.multiple_of(part * half + t * 128, 128), 128)
            k, v = qkv[1, part, :, at], qkv[2, part, :, at]
            d_k, d_v = jnp.zeros((tokens, 128), WIDE), jnp.zeros((tokens, 128), WIDE)
            for i in range(tokens // qb):
                rows = pl.ds(i * qb, qb)
                q = qkv[0, part, rows, at]
                dc = clip_mid[rows, wide_at]
                prod = dc.astype(WIDE) * ctx[rows, wide_at]
                found = stats[rows, :]
                d_q = jnp.zeros((qb, 128), WIDE)
                for h in range(2):
                    kz = jnp.where(in_head[h], k, jnp.zeros_like(k))
                    vz = jnp.where(in_head[h], v, jnp.zeros_like(v))
                    qz = jnp.where(in_head[h], q, jnp.zeros_like(q))
                    dcz = jnp.where(in_head[h], dc, jnp.zeros_like(dc))
                    mean = jnp.sum(jnp.where(in_head[h], prod, 0.0), axis=-1, keepdims=True)
                    total = jnp.sum(jnp.where(lane == (part * 6 + t * 2 + h), found, 0.0), axis=-1, keepdims=True)
                    p = jnp.exp(dot_nt(q, kz) + bias[rows, :] - total)
                    d_s = (p * (dot_nt(dc, vz) - mean)).astype(LOW)
                    d_q = d_q + dot(d_s, kz)
                    d_k = d_k + dot_tn(d_s, qz)
                    d_v = d_v + dot_tn(p.astype(LOW), dcz)
                qkv[0, part, rows, at] = (d_q * (HD ** -0.5)).astype(LOW)
            qkv[1, part, :, at] = d_k.astype(LOW)
            qkv[2, part, :, at] = d_v.astype(LOW)
            return carry

        lax.fori_loop(0, half // 128, pair, 0)

    if upto >= 4:
        step(DOWN0 + 1, 1)
        step(DOWN0 + 2, 1)
        attend_back(other)
        for i in range(2):
            m = QKV0 + i
            scatter.slot_free(m)
            store_wide(cs_w, ((5 + i) % 2,), dot_tn(qkv[i, other], clip_in[...]), MESSAGES[m][2])
            scatter.send_core(m)
        step(IN0, 1)
        step(IN0 + 1, 1)
        attend_back(mp)
        for i in range(2):
            m = QKV0 + i
            store_wide(acc_w, (5 + i,), dot_tn(qkv[i, mp], clip_in[...]), MESSAGES[m][2])
            step(m, 0)
        m = QKV0 + 2
        scatter.slot_free(m)
        store_wide(cs_w, (7 % 2,), dot_tn(qkv[2, other], clip_in[...]), MESSAGES[m][2])
        scatter.send_core(m)
        store_wide(acc_w, (7,), dot_tn(qkv[2, mp], clip_in[...]), MESSAGES[m][2])
        step(m, 0)
        for r, j in ((10, 0), (11, 2)):
            for part in range(2):
                sm[r : r + 1, half * part : half * part + half] = jnp.sum(qkv[j, part].astype(WIDE), axis=0, keepdims=True)

    if upto >= 5:
        for n, (part, j) in enumerate([(part, j) for part in range(2) for j in range(3)]):
            back = dot_nt(qkv[j, part], wqkv[part, j])
            if n == 0:
                h2[...] = back
            else:
                h2[...] += back

        def token_rows(i, carry):
            rows = rows_at(i)
            th = jnp.tanh(tok[rows, :].astype(WIDE) * i0)
            d_h1[rows, :] += h2[rows, :] * (1.0 - th * th)
            return carry

        lax.fori_loop(0, tokens // rb, token_rows, 0)
        tok_copy = pltpu.make_async_copy(d_h1, gtok_h, loc_sem.at[7])
        tok_copy.start()

        is_peak = lax.broadcasted_iota(jnp.int32, sm.shape, 0) == 12

        def small_copy(k):
            return pltpu.make_async_remote_copy(
                src_ref=sm,
                dst_ref=sm_r.at[k],
                send_sem=ssend.at[k],
                recv_sem=srecv.at[k],
                device_id=partners[k],
                device_id_type=MESH,
            )

        def small_end(k):
            small_copy(k).wait()
            sm[...] = jnp.where(is_peak, jnp.maximum(sm[...], sm_r[k]), sm[...] + sm_r[k])
            if k + 1 < len(partners):
                small_copy(k + 1).start()

        small_copy(0).start()
        for k in range(len(partners)):
            small_end(k)
        drain()

        per = width // (2 * n_dp)
        me = dp * 2 + mp
        sums = sm[...]
        out = pltpu.roll(sums, (width - per * me) % width, 1)[:, :128]
        qv_out = pltpu.roll(sums, (width - (mp * half + per * dp)) % width, 1)[:, :128]
        wide_at = 4 * per * me
        in_rows = pltpu.roll(sums, (width - wide_at % width) % width, 1)[:, :128]
        r_iota = lax.broadcasted_iota(jnp.int32, out.shape, 0)
        in_row = jnp.sum(jnp.where(r_iota == 3 + wide_at // width, in_rows, 0.0), axis=0, keepdims=True)
        out = jnp.where((r_iota == 10) | (r_iota == 11), qv_out, out)
        out = jnp.where(r_iota == 3, in_row, out)
        small_o[...] = out
        small_o[12:13, 0:4] = MOMENTUM * act_v[...] + (1.0 - MOMENTUM) * sums[12:13, 0:4]
        tok_copy.wait()
    else:
        lay_copy.wait() if upto < 3 else None
        drain()


def per_device(n_dp, upto, tokens, seg_ids, fill_len, qkv_weight, qv_bias, out_weight, out_bias, norm1_gain, norm1_bias, in_weight, in_bias,
               down_weight, down_bias, norm2_gain, norm2_bias, act_range, cotangent):
    n_tok, width = tokens.shape
    hidden = in_weight.shape[1]
    half = width // 2
    n_low = max(1, n_dp // 16)
    any_, vmem = pl.BlockSpec(memory_space=pl.ANY), pl.BlockSpec(memory_space=pltpu.VMEM)
    smem = pl.BlockSpec(memory_space=pltpu.SMEM)
    chunk = width // 32
    shape = jax.ShapeDtypeStruct
    low = lambda *s: pltpu.VMEM(s, LOW)
    wide = lambda *s: pltpu.VMEM(s, WIDE)
    dma = lambda *s: pltpu.SemaphoreType.DMA(s)
    n_partners = n_dp.bit_length()
    n_wide = N_MSG - 3
    outs = pl.pallas_call(
        functools.partial(kernel, n_dp, n_low, upto),
        out_shape=(
            shape((n_tok, width), LOW),
            shape((n_tok, width), WIDE),
            shape((3, chunk, width), WIDE),
            shape((chunk, width), WIDE),
            shape((chunk, hidden), WIDE),
            shape((4 * chunk, width), WIDE),
            shape((16, 128), WIDE),
        ),
        in_specs=[any_, vmem, smem, any_, vmem, any_, vmem, vmem, vmem, any_, vmem, any_, vmem, vmem, vmem, vmem, any_],
        out_specs=(any_, any_, vmem, vmem, vmem, vmem, vmem),
        scratch_shapes=[
            low(n_tok, width), low(n_tok, width), low(2, 3, width, half), wide(2, 2, half), low(width, width), low(width, hidden), low(hidden, width),
            low(n_tok, width), low(3, 2, n_tok, half), wide(n_tok, n_tok), wide(n_tok, width), wide(n_tok, 128), low(2, half, n_tok),
            wide(n_tok, width), low(n_tok, width), low(2, half, n_tok), low(2, 3, 16, 32, n_tok), low(n_tok, hidden),
            wide(n_tok, width), wide(n_tok, width), wide(16, width), wide(n_partners, 16, width),
            low(3, 16, 32, width), low(n_wide, 16, 48, half), low(2, 16, 32, width), low(2, 16, 48, half), low(3, 16, 32, width), low(n_wide, 16, 48, half),
            *(low(3, 16 >> k, 32, width) for k in range(1, 5)), *(low(n_wide, 16 >> k, 48, half) for k in range(1, 5)),
            dma(8), dma(2), dma(2), dma(N_MSG, 5), dma(N_MSG, 5), dma(n_partners), dma(n_partners),
        ],
        compiler_params=pltpu.CompilerParams(collective_id=0, has_side_effects=True, vmem_limit_bytes=64 * 2**20 - 2**16),
        cost_estimate=pl.CostEstimate(flops=25_000_000_000, bytes_accessed=24_000_000, transcendentals=12_000_000),
    )(
        tokens, seg_ids, fill_len, jnp.transpose(qkv_weight, (1, 0, 2)), qv_bias, out_weight, out_bias.reshape(1, width), norm1_gain.reshape(1, width),
        norm1_bias.reshape(1, width), in_weight, in_bias.reshape(1, hidden), down_weight, down_bias.reshape(1, width), norm2_gain.reshape(1, width),
        norm2_bias.reshape(1, width), act_range.reshape(1, 4), cotangent,
    )
    layer_out, grad_tokens, qkv_sum, sum_out, sum_in, sum_down, small = outs
    if n_low > 1:
        groups = [[top * n_low + low_ for low_ in range(n_low)] for top in range(16)]
        moves = [((top * n_low + i) * 2 + core, n_low * (2 * top + core) + i) for top in range(16) for i in range(n_low) for core in range(2)]

        def spread(v, dim):
            return lax.psum_scatter(v, "dp", scatter_dimension=dim, axis_index_groups=groups, tiled=True)

        qkv_sum = spread(qkv_sum, 1)
        sum_out, sum_in, sum_down = (lax.ppermute(spread(v, 0), ("dp", "mp"), moves) for v in (sum_out, sum_in, sum_down))
    per = width // (2 * n_dp)
    row = lambda i: small[i, :per]
    return (
        layer_out,
        grad_tokens,
        jnp.transpose(qkv_sum, (2, 0, 1)),
        small[10:12, :per],
        sum_out,
        row(0),
        row(1),
        row(2),
        sum_in,
        small[3, : 4 * per],
        sum_down,
        row(7),
        row(8),
        row(9),
        small[12, :4],
    )


def solution(mesh, upto=5):
    n_dp = mesh.shape["dp"]
    both, copies = P(("dp", "mp")), P()
    rows = P(("dp", "mp"), None)
    return jax.shard_map(
        functools.partial(per_device, n_dp, upto),
        mesh=mesh,
        in_specs=(
            rows, P("dp", None), P("dp"), P(None, None, "mp"), P(None, "mp"),
            *([copies] * 11), rows,
        ),
        out_specs=(
            rows, rows, P(None, None, ("mp", "dp")), P(None, ("mp", "dp")), rows, both, both, both, rows, both, rows, both, both, both, copies,
        ),
        check_vma=False,
    )
```

time: 704 us -> 158 us (0.22); the launches traced: 695 us -> 157 us
  waiting for transfers between devices: 363 us -> 0 us
  Pallas kernels: 0 us -> 138 us
  blocking collectives: 130 us -> 0 us
  matrix products: 104 us -> 0 us
  other arithmetic: 32.2 us -> 0 us
  local copies, waits for them, and re-layouts: 49.6 us -> 18.7 us
  between operations: 15.8 us -> 0.68 us
    reduce_scatter x4 -> x0, waiting for transfers between devices: 355 us -> none  [the longest x1 142 us: per_device(): lax.psum_scatter(grad_down, ('dp', 'mp'), scatter_dimension=0, tiled=True)]
    pallas_call x0 -> x1, Pallas kernels: none -> 138 us  [per_device(): pl.pallas_call(functools.partial(kernel, n_dp, n_low, upto), out_shape=(s...]
    dot_general x18 -> x0, matrix products: 104 us -> none  [the longest x1 20.4 us: per_device(): jnp.dot(clip_mid, in_weight, preferred_element_type=wide_type) + in_bias]
    unnamed x2 -> x0, blocking collectives: 82.8 us -> none
    pmax x1 -> x0, blocking collectives: 36.8 us -> none  [per_device(): peaks = lax.pmax(local_peaks, ('dp', 'mp'))]
    unnamed x90 -> x16, local copies, waits for them, and re-layouts: 27.8 us -> 5.97 us
    convert_element_type x6 -> x0, other arithmetic: 15.5 us -> none  [the longest x1 7.42 us: per_device(): d_scores = (re_probs * (d_probs - row_dot)).astype(low_type)]
    all_to_all x2 -> x0, blocking collectives: 9.93 us -> none  [the longest x1 5.58 us: per_device(): lax.all_to_all(d_mixed_tok, 'mp', split_axis=1, concat_axis=0, tiled=True)]
  transfers between devices with their start and end apart: 6 -> 0, of which waited for: 4 -> 0; matrix products, arithmetic and copies ran while one was open for 10% -> 0% of each run, Pallas kernels for 0% -> 0%
where the time goes in v1:
time: 158 us; the launch traced here: 157 us
  Pallas kernels  138 us (87%)
  local copies, waits for them, and re-layouts  18.7 us (12%)
    pallas_call x1, Pallas kernels, per_device(): pl.pallas_call(functools.partial(kernel, n_dp, n_low, upto), out_shape=(s...  138 us
    unnamed x16, local copies, waits for them, and re-layouts  5.97 us

profile of v1, /device:TPU:0, one launch (start us, length us, event | category | flops | bytes accessed | tf_op | source)
XLA Modules:
  0.0 157.4 jit_solution(707041147842017362)
XLA Ops:
  0.6 1.3 reshape.54.outb_v
  1.9 1.3 reshape.55.g1_v
  3.2 1.3 reshape.56.b1_v
  4.4 1.3 reshape.58.downb_v
  5.7 1.3 reshape.59.g2_v
  7.0 1.3 reshape.60.b2_v
  8.2 138.1 %shard_map.280 = (bf16[512,768]{1,0:T(8,128)(2,1)}, f32[512,768]{1,0:T(8,128)}, f32[3,24,768]{2,1,0:T(8,128)}, f32[24,768]{1,0:T(8,128)}, f32[24,3072]{1,0:T(8,1...) custom-call(bf16[512,768]{1,0:T(8,128)(2,1)} %tok_h.1, s32[2,512]{1,0:T(2,128)} %seg_v.1, s32[2]{0:T(128)} %fill_s.1, ...), custom_call_target="tpu_custom_call" | custom-call | flops 24999999488 | bytes 24000000 | tf_op jit(solution)/shard_map/pallas_call | solution.py:618
  146.3 0.0 copy-start
  146.3 1.3 slice_bitcast_fusion
  147.6 1.2 slice_bitcast_fusion.4
  148.8 1.2 slice.27
  150.1 1.3 slice_bitcast_fusion.1
  151.4 2.1 %copy.38 = bf16[512,768]{1,0:T(8,128)(2,1)} copy(bf16[512,768]{1,0:T(8,128)(2,1)} %get-tuple-element.50) | data formatting | bytes 1572864
  153.5 0.0 copy-done
  153.5 0.0 copy-start.3
  153.5 0.0 copy-start.4
  153.5 0.0 copy-start.2
  153.5 0.0 copy-start.1
  153.5 1.1 copy.39
  154.7 0.0 copy-done.3
  154.7 0.7 copy.40
  155.3 0.0 copy-done.4
  155.3 0.6 copy.41
  156.0 0.0 copy-done.2
  156.0 0.7 copy.42
  156.7 0.0 copy-done.1
  156.7 0.7 copy.43
Async XLA Ops:
  146.3 7.2 %copy-start = (f32[512,768]{1,0:T(8,128)S(1)}, f32[512,768]{1,0:T(8,128)}, u32[]{:S(2)}) copy-start(f32[512,768]{1,0:T(8,128)} %get-tuple-element.51) | copy-start | bytes 4718596
  153.5 1.2 copy-start.3
  153.5 1.9 %copy-start.4 = (f32[24,768]{1,0:T(8,128)S(1)}, f32[24,768]{1,0:T(8,128)}, u32[]{:S(2)}) copy-start(f32[24,768]{1,0:T(8,128)} %get-tuple-element.54) | copy-start | bytes 221188
  153.5 2.5 %copy-start.2 = (f32[24,3072]{1,0:T(8,128)S(1)}, f32[24,3072]{1,0:T(8,128)}, u32[]{:S(2)}) copy-start(f32[24,3072]{1,0:T(8,128)} %get-tuple-element.58) | copy-start | bytes 884740
  153.5 3.2 %copy-start.1 = (f32[96,768]{1,0:T(8,128)S(1)}, f32[96,768]{1,0:T(8,128)}, u32[]{:S(2)}) copy-start(f32[96,768]{1,0:T(8,128)} %get-tuple-element.60) | copy-start | bytes 884740
